TPU v7x, 32 devices: a whole 2x2x4 slice. The times are simulated.
32 devices in a mesh: row: 8 (over y, x, core), col: 4 (over z).
Axes of the slice: x: 2, y: 2, z: 4, core: 2. Of those that a mesh axis runs over, the one named last changes fastest.
Arguments:
- coeffs: bfloat16 [8192, 2048], P('row', 'col'), may hold values from -1.5 to 1.5
- basis_values: bfloat16 [32, 512, 512], P(('row', 'col')), may hold values from -1 to 1
- point_weights: float32 [32, 512], P(('row', 'col')), may hold values from 0.05 to 1
- point_counts: int32 [32], P(('row', 'col')), may hold values from 1 to 512, as said below
- func_lists: int32 [32, 512], P(('row', 'col')), may hold values from 0 to 8191, as said below
Outputs:
- density: bfloat16 [8192, 8192], P('col', 'row')
- potential: float32 [8192, 8192], P('col', 'row')
Inputs may be any that keep to these rules, and one draw needn't show every extreme that they name: `func_lists`: A batch held by device index d of row+col has its functions in the three row-axis blocks (d // 4 - 1) mod 8, d // 4 and its successor, each block 1024 functions, indices taken modulo 8192; a list holds distinct indices. `point_counts`: some batch has all 512 points live in every draw.
All inputs are finite; a program needn't handle non-finite values.
Results may differ from a plain program's by a relative error of at most 0.006.
Values may be sent and summed in bfloat16 or wider, within the bound.
No kernel may reach another device: no remote copies, remote signals or barrier semaphores. Data moves between devices by JAX's collectives and lax.ppermute only.
A program may use at most 128 MiB of HBM per device.

v0:
```python
import jax
import jax.numpy as jnp
from jax import lax
from jax.sharding import PartitionSpec as P

slater_coef = 0.9847450218426965


def from_root(array, axis, root):
    mine = lax.axis_index(axis) == root
    return lax.psum(jnp.where(mine, array, jnp.zeros_like(array)), axis)


def with_halo(array, sides, width):
    for axis, dim in sides:
        count, length = (lax.axis_size(axis), array.shape[dim])
        up = [(i, (i + 1) % count) for i in range(count)]
        down = [(j, i) for i, j in up]
        last = lax.slice_in_dim(array, length - width, length, axis=dim)
        first = lax.slice_in_dim(array, 0, width, axis=dim)
        before = lax.ppermute(last, axis, up)
        after = lax.ppermute(first, axis, down)
        array = jnp.concatenate([before, array, after], axis=dim)
    return array


def shifted(array, axis, by):
    count = lax.axis_size(axis)
    return lax.ppermute(array, axis, [(i, (i + by) % count) for i in range(count)])


def exchange_potential(density_pts):
    return -slater_coef * jnp.power(density_pts + 1.0, 1.0 / 3.0)


def on_device(coeffs, basis_values, point_weights, point_counts, func_lists):
    row_devices = lax.axis_size("row")
    col_devices = lax.axis_size("col")
    tile_rows = coeffs.shape[0]
    basis_total = tile_rows * row_devices
    col_width = basis_total // col_devices
    window = 3 * tile_rows
    row_id = lax.axis_index("row")
    col_id = lax.axis_index("col")
    own_rows = lax.all_gather(coeffs, "col", axis=1, tiled=True)
    blocks_per_col = row_devices // col_devices
    first_block = col_id * blocks_per_col

    def add_panel(block_step, dens_rows):
        row_panel = from_root(own_rows, "row", first_block + block_step)
        tile_part = 2.0 * lax.dot_general(
            row_panel, own_rows, (((1,), (1,)), ((), ())), preferred_element_type=jnp.float32
        )
        return lax.dynamic_update_slice_in_dim(dens_rows, tile_part, block_step * tile_rows, 0)

    density = lax.fori_loop(
        0, blocks_per_col, add_panel, jnp.zeros((col_width, tile_rows), jnp.float32)
    ).astype(jnp.bfloat16)
    strip_cols = with_halo(density, (("row", 1),), tile_rows)
    window_start = (row_id - 1) % row_devices * tile_rows
    window_global = (window_start + jnp.arange(window, dtype=jnp.int32)) % basis_total
    full_rows = lax.all_gather(strip_cols, "col", axis=0, tiled=True)
    dens_window = jnp.take(full_rows, window_global, axis=0)
    npoints = basis_values.shape[1]
    nlisted = basis_values.shape[2]
    block_rows = min(512, npoints)
    window_slots = jnp.arange(window, dtype=jnp.int32)
    local_index = (func_lists[0] - window_start) % basis_total
    selector = window_slots[:, None] == local_index[None, :]
    select_half = selector.astype(jnp.bfloat16)
    select_full = selector.astype(jnp.float32)
    picked_rows = lax.dot_general(
        select_half, dens_window, (((0,), (0,)), ((), ())), preferred_element_type=jnp.float32
    ).astype(jnp.bfloat16)
    dens_block = jnp.dot(picked_rows, select_half, preferred_element_type=jnp.float32).astype(
        jnp.bfloat16
    )
    basis_block = basis_values[0]
    weights = point_weights[0]
    count_pts = point_counts[0]
    block_count = (count_pts + block_rows - 1) // block_rows

    def add_block(
        block_id,
        pot_block,
        basis_block=basis_block,
        weights=weights,
        count_pts=count_pts,
        dens_block=dens_block,
    ):
        start_row = block_id * block_rows
        projected = jnp.dot(basis_block, dens_block, preferred_element_type=jnp.float32)
        density_pts = jnp.sum(projected * basis_block.astype(jnp.float32), axis=1)
        is_live = start_row + jnp.arange(block_rows, dtype=jnp.int32) < count_pts
        pot_pts = jnp.where(is_live, weights * exchange_potential(density_pts), jnp.float32(0.0))
        scaled = (basis_block.astype(jnp.float32) * pot_pts[:, None]).astype(jnp.bfloat16)
        return pot_block + lax.dot_general(
            basis_block, scaled, (((0,), (0,)), ((), ())), preferred_element_type=jnp.float32
        )

    pot_block = lax.fori_loop(0, block_count, add_block, jnp.zeros((nlisted, nlisted), jnp.float32))
    spread_cols = lax.dot_general(
        pot_block,
        select_full,
        (((1,), (1,)), ((), ())),
        precision=lax.Precision.HIGHEST,
        preferred_element_type=jnp.float32,
    )
    placed = jnp.dot(
        select_full,
        spread_cols,
        precision=lax.Precision.HIGHEST,
        preferred_element_type=jnp.float32,
    )
    summed = lax.psum(placed.astype(jnp.bfloat16), "col").astype(jnp.float32)
    own_global = col_id * col_width + jnp.arange(col_width, dtype=jnp.int32)
    window_rows = (own_global - window_start) % basis_total
    is_inside = window_rows < window
    row_select = jnp.where(
        is_inside[:, None],
        jnp.take(summed, jnp.clip(window_rows, 0, window - 1), axis=0),
        jnp.float32(0.0),
    )
    below_part = row_select[:, :tile_rows]
    middle = row_select[:, tile_rows : 2 * tile_rows]
    above_part = row_select[:, 2 * tile_rows :]
    potential = (
        middle
        + shifted(below_part.astype(jnp.bfloat16), "row", -1).astype(below_part.dtype)
        + shifted(above_part.astype(jnp.bfloat16), "row", 1).astype(above_part.dtype)
    )
    return (density, potential)


def solution(mesh):
    in_specs = (
        P("row", "col"),
        P(("row", "col"), None, None),
        P(("row", "col"), None),
        P(("row", "col")),
        P(("row", "col"), None),
    )
    out_specs = (P("col", "row"), P("col", "row"))
    return jax.shard_map(
        on_device, mesh=mesh, in_specs=in_specs, out_specs=out_specs, check_vma=False
    )
```

profile of v0, /device:TPU:0, one launch (start us, length us, event | category | flops | bytes accessed | tf_op | source)
XLA Modules:
  0.0 2186.0 jit_solution(1345635204208117691)
XLA Ops:
  7.2 0.0 all-gather.3.cloned.1.call-start
  7.2 0.7 all-gather.3.cloned.1.call-update
  7.9 85.2 %all-gather.3.cloned.1.call-done = bf16[1024,2048]{1,0:T(8,128)(2,1)} async-done(((bf16[1024,512]{1,0:T(8,128)(2,1)}), bf16[1024,2048]{1,0:T(8,128)(2,1)}) %all-gather.3.cloned.1.call-update) | async-done | bytes 4194320 | tf_op jit(solution)/shard_map/all_gather | solution.py:45
  93.1 2.5 broadcast_in_dim.46
  95.6 189.4 %while.27 = (s32[]{:T(128)}, bf16[2048,1024]{1,0:T(8,128)(2,1)}, s32[]{:T(128)}, bf16[1024,2048]{1,0:T(8,128)(2,1)}, s32[]{:T(128)}, /*index=5*/s32[]{:T(128)}, s32[]{:T(128)}, s32[]{:T(128)}, u32[]{:T(128)}, u32[]{:T(128)}) while((s32[]{:T(128)}, bf16[2048,1024]{1,0:T(8,128)(2,1)}, s32[]{:T(128)}, bf16[1024,2048]{1,0:T(8,128)(2,1)}, ...), condition=%wide.region_2.3_spmd, body=%wide.region_0.2_spmd.sunk | while | flops 4300210176 | bytes 46137588 | solution.py:56
  95.6 0.0 all-reduce.5.cloned.1.call-start
  95.6 4.5 broadcast_select_fusion.2
  100.1 0.0 all-reduce.5.cloned.1.call-update
  100.1 80.1 %all-reduce.5.cloned.1.call-done = bf16[1024,2048]{1,0:T(8,128)(2,1)} async-done(((bf16[1024,2048]{1,0:T(8,128)(2,1)}), bf16[1024,2048]{1,0:T(8,128)(2,1)}) %all-reduce.5.cloned.1.call-update) | async-done | bytes 4194320 | tf_op jit(solution)/shard_map/while/body/eval_jaxpr/psum | solution.py:11
  180.2 9.3 multiply_dynamic-update-slice_fusion.2
  189.5 2.3 broadcast_select_fusion.2
  191.8 0.0 all-reduce.5.cloned.1.call-update
  191.8 83.8 %all-reduce.5.cloned.1.call-done = bf16[1024,2048]{1,0:T(8,128)(2,1)} async-done(((bf16[1024,2048]{1,0:T(8,128)(2,1)}), bf16[1024,2048]{1,0:T(8,128)(2,1)}) %all-reduce.5.cloned.1.call-update) | async-done | bytes 4194320 | tf_op jit(solution)/shard_map/while/body/eval_jaxpr/psum | solution.py:11
  275.6 9.3 multiply_dynamic-update-slice_fusion.2
  285.0 0.0 all-gather.5.cloned.1.call-start
  285.0 0.0 collective-permute-start
  285.0 2.6 collective-permute-start.1
  287.6 90.4 %collective-permute-done = bf16[2048,1024]{1,0:T(8,128)(2,1)S(1)} collective-permute-done((bf16[2048,1024]{1,0:T(8,128)(2,1)}, bf16[2048,1024]{1,0:T(8,128)(2,1)S(1)}, u32[]{:S(2)}, u32[]{:S(2)}) %collective-permute-start) | collective-permute-done | bytes 4194336 | tf_op jit(solution)/shard_map/ppermute | solution.py:21
  378.0 0.0 collective-permute-done.1
  378.0 7.7 pad_maximum_fusion
  385.7 0.0 all-gather.5.cloned.1.call-update
  385.7 0.2 all-reduce.3.cloned.1.call-start
  386.7 0.0 copy-done.3
  386.7 0.1 compare_select_fusion
  386.8 1.3 iota_compare_fusion.19
  388.0 834.2 %all-gather.5.cloned.1.call-done = bf16[8192,3072]{1,0:T(8,128)(2,1)} async-done(((bf16[2048,3072]{1,0:T(8,128)(2,1)}), bf16[8192,3072]{1,0:T(8,128)(2,1)}) %all-gather.5.cloned.1.call-update) | async-done | bytes 50331664 | tf_op jit(solution)/shard_map/all_gather | solution.py:62
  1222.3 85.3 %gather_fusion = bf16[3072,3072]{1,0:T(8,128)(2,1)} fusion(bf16[8192,3072]{1,0:T(8,128)(2,1)} %all-gather.5.cloned.1.call-done, s32[3072]{0:T(1024)S(1)} %broadcast_clamp_fusion), kind=kCustom, calls=%fused_computation | custom fusion | bytes 37761024 | tf_op jit(solution)/shard_map/jit(_take)/gather | solution.py:63
  1307.6 16.2 fusion.19
  1323.8 0.5 fusion.22
  1324.4 0.1 broadcast_in_dim.49
  1324.5 1.5 while.28
  1324.5 0.7 multiply_select_fusion.2
  1325.2 0.6 fusion.55
  1326.0 10.3 fusion.7
  1336.3 33.2 %convolution_convert_fusion = bf16[3072,3072]{1,0:T(8,128)(2,1)} fusion(f32[512,3072]{1,0:T(8,128)S(1)} %fusion.7, s32[512]{0:T(512)S(1)} %bitcast.41), kind=kOutput, calls=%fused_computation.14 | convolution fusion | flops 57993068544 | bytes 25167872 | tf_op jit(solution)/shard_map/dot_general | solution.py:109
  1369.5 0.0 all-reduce.3.cloned.1.call-update
  1369.6 0.1 compare_select_fusion.3
  1369.6 627.8 %all-reduce.3.cloned.1.call-done = bf16[3072,3072]{1,0:T(8,128)(2,1)} async-done(((bf16[3072,3072]{1,0:T(8,128)(2,1)}), bf16[3072,3072]{1,0:T(8,128)(2,1)}) %all-reduce.3.cloned.1.call-update) | async-done | bytes 18874384 | tf_op jit(solution)/shard_map/psum | solution.py:115
  1997.4 21.0 convert_element_type.48
  2018.4 34.0 %gather_fusion.1 = f32[2048,3072]{1,0:T(8,128)} fusion(f32[3072,3072]{1,0:T(8,128)} %convert_element_type.48, s32[2048]{0:T(1024)S(1)} %broadcast_clamp_fusion.1), kind=kCustom, calls=%fused_computation.1 | custom fusion | bytes 50339840 | tf_op jit(solution)/shard_map/jit(_take)/gather | solution.py:121
  2052.5 19.3 fusion.36
  2071.8 0.9 fusion.37
  2072.7 1.9 collective-permute-start.2
  2074.5 0.0 collective-permute-start.3
  2074.5 90.1 %collective-permute-done.2 = bf16[2048,1024]{1,0:T(8,128)(2,1)S(1)} collective-permute-done((bf16[2048,1024]{1,0:T(8,128)(2,1)S(1)}, bf16[2048,1024]{1,0:T(8,128)(2,1)S(1)}, u32[]{:S(2)}, u32[]{:S(2)}) %collective-permute-start.2) | collective-permute-done | bytes 4194336 | tf_op jit(solution)/shard_map/ppermute | solution.py:29
  2164.7 1.9 collective-permute-done.3
  2166.5 2.0 copy-done.1
  2168.5 10.5 fusion.6
  (12 shorter events, 0.1 us)
Async XLA Ops:
  7.2 85.9 %all-gather.3.cloned.1.call-start = ((), (), s32[]{:S(2)}) async-start(), calls=%async_computation | async-start | bytes 5242880 | tf_op jit(solution)/shard_map/all_gather | solution.py:45
  95.6 84.6 %all-reduce.5.cloned.1.call-start = ((), (), s32[]{:S(2)}) async-start(), calls=%async_computation.3 | async-start | bytes 8388608 | tf_op jit(solution)/shard_map/while/body/eval_jaxpr/psum | solution.py:11
  189.5 86.1 %all-reduce.5.cloned.1.call-start = ((), (), s32[]{:S(2)}) async-start(), calls=%async_computation.3 | async-start | bytes 8388608 | tf_op jit(solution)/shard_map/while/body/eval_jaxpr/psum | solution.py:11
  285.0 937.3 %all-gather.5.cloned.1.call-start = ((), (), s32[]{:S(2)}) async-start(), calls=%async_computation.1 | async-start | bytes 62914560 | tf_op jit(solution)/shard_map/all_gather | solution.py:62
  285.0 93.1 %collective-permute-start = (bf16[2048,1024]{1,0:T(8,128)(2,1)}, bf16[2048,1024]{1,0:T(8,128)(2,1)S(1)}, u32[]{:S(2)}, u32[]{:S(2)}) collective-permute-start(bf16[2048,1024]{1,0:T(8,128)(2,1)} %get-tuple-element.217), channel_id=1, source_target_pairs={{0,4},{4,8},{8,12},{12,16},{16,20},{20,24},{24,28},{28,0},{1,5},{5... | collective-permute-start | bytes 12582920 | tf_op jit(solution)/shard_map/ppermute | solution.py:21
  285.0 93.1 %collective-permute-start.1 = (bf16[2048,1024]{1,0:T(8,128)(2,1)}, bf16[2048,1024]{1,0:T(8,128)(2,1)S(1)}, u32[]{:S(2)}, u32[]{:S(2)}) collective-permute-start(bf16[2048,1024]{1,0:T(8,128)(2,1)} %get-tuple-element.217), channel_id=1, source_target_pairs={{4,0},{8,4},{12,8},{16,12},{20,16},{24,20},{28,24},{0,28},{5,1},{9... | collective-permute-start | bytes 12582920 | tf_op jit(solution)/shard_map/ppermute | solution.py:22
  385.7 1.0 copy-start.3
  385.7 1611.7 %all-reduce.3.cloned.1.call-start = ((), (), s32[]{:S(2)}) async-start(), calls=%async_computation.2 | async-start | bytes 37748736 | tf_op jit(solution)/shard_map/psum | solution.py:115
  1307.6 16.2 copy-start
  1307.6 16.9 copy-start.2
  2072.7 92.0 %collective-permute-start.2 = (bf16[2048,1024]{1,0:T(8,128)(2,1)S(1)}, bf16[2048,1024]{1,0:T(8,128)(2,1)S(1)}, u32[]{:S(2)}, u32[]{:S(2)}) collective-permute-start(bf16[2048,1024]{1,0:T(8,128)(2,1)S(1)} %get-tuple-element.243), channel_id=1, source_target_pairs={{0,28},{4,0},{8,4},{12,8},{16,12},{20,16},{24,20},{28,24},{1,29},{... | collective-permute-start | bytes 12582920 | tf_op jit(solution)/shard_map/ppermute | solution.py:29
  2074.5 92.0 %collective-permute-start.3 = (bf16[2048,1024]{1,0:T(8,128)(2,1)S(1)}, bf16[2048,1024]{1,0:T(8,128)(2,1)S(1)}, u32[]{:S(2)}, u32[]{:S(2)}) collective-permute-start(bf16[2048,1024]{1,0:T(8,128)(2,1)S(1)} %get-tuple-element.244), channel_id=1, source_target_pairs={{0,4},{4,8},{8,12},{12,16},{16,20},{20,24},{24,28},{28,0},{1,5},{5... | collective-permute-start | bytes 12582920 | tf_op jit(solution)/shard_map/ppermute | solution.py:29
  2166.5 2.0 copy-start.1
Sparse Core Ops, SparseCore 0:
  9.6 83.4 all-gather.2
  100.6 79.5 all-reduce.4
  194.5 81.0 all-reduce.4
  385.8 836.3 all-gather.4
  1369.7 627.6 all-reduce.2
where the time goes:
time: 2190 us
  waiting for transfers between devices  1890 us (86%)
  local copies, waits for them, and re-layouts  125 us (6%)
  matrix products  79.4 us (4%)
  other arithmetic  67.4 us (3%)
    all_gather x1, waiting for transfers between devices, on_device(): full_rows = lax.all_gather(strip_cols, 'col', axis=0, tiled=True)  834 us
    psum x1, waiting for transfers between devices, on_device(): summed = lax.psum(placed.astype(jnp.bfloat16), 'col').astype(jnp.float32)  628 us
    psum x2, waiting for transfers between devices, from_root(): return lax.psum(jnp.where(mine, array, jnp.zeros_like(array)), axis)  164 us
    ppermute x2, waiting for transfers between devices, shifted(): lax.ppermute(array, axis, [(i, (i + by) % count) for i in range(count)])  92 us
    ppermute x1, waiting for transfers between devices, with_halo(): before = lax.ppermute(last, axis, up)  90.4 us
    gather x1, local copies, waits for them, and re-layouts, on_device(): dens_window = jnp.take(full_rows, window_global, axis=0)  85.3 us
    all_gather x1, waiting for transfers between devices, on_device(): own_rows = lax.all_gather(coeffs, 'col', axis=1, tiled=True)  85.2 us
  transfers between devices with their start and end apart: 9, of which 8 were waited for; matrix products, arithmetic and copies ran while one was open for 0% of the time, Pallas kernels for 0%

commit v1 on v0

v1 whole, which is shorter than its diff:
```python
import functools

import jax
import jax.numpy as jnp
from jax import lax
from jax.experimental import pallas as pl
from jax.experimental.pallas import tpu as pltpu
from jax.sharding import PartitionSpec as P

slater_coef = 0.9847450218426965
both = ("row", "col")
extra = 16
lanes = 128
vmem_bytes = 52 * 1024 * 1024


def latin(a, b, n):
    if n & (n - 1) == 0:
        return a ^ b
    return (b - a + n) % n


def ring(x, n, by=1):
    return lax.ppermute(x, "col", [(i, (i + by) % n) for i in range(n)])


def row_shift(x, n, by):
    return lax.ppermute(x, "row", [(i, (i + by) % n) for i in range(n)])


def as_column(row_vec, width=lanes):
    return jnp.broadcast_to(row_vec, (width, row_vec.shape[1])).T


def list_of(b_ref, npts):
    hi = b_ref[npts : npts + 1, :].astype(jnp.float32)
    lo = b_ref[npts + 1 : npts + 2, :].astype(jnp.float32)
    return hi * 128.0 + lo


def weight_of(b_ref, npts):
    w1 = b_ref[npts + 2 : npts + 3, :].astype(jnp.float32)
    w2 = b_ref[npts + 3 : npts + 4, :].astype(jnp.float32)
    w3 = b_ref[npts + 4 : npts + 5, :].astype(jnp.float32)
    return (w1 + w2) + w3


def one_hot_columns(column, base, width, out_ref):
    for at in range(0, width, lanes):
        spot = lax.broadcasted_iota(jnp.int32, column.shape, 1) + (base + at)
        out_ref[:, at : at + lanes] = jnp.where(column == spot, 1.0, 0.0).astype(jnp.bfloat16)


def rho_kernel(n_col, n_row, npts, where_ref, *refs):
    b_refs, (c_before, c_own, c_after, out_ref, pick_ref) = refs[:n_col], refs[n_col:]
    tile = c_own.shape[0]
    total = tile * n_row
    row, col = where_ref[0], where_ref[1]
    start = lax.rem(row + n_row - 1, n_row) * tile
    for k, b_ref in enumerate(b_refs):
        index = list_of(b_ref, npts).astype(jnp.int32) - start
        index = jnp.where(index < 0, index + total, index)
        one_hot_columns(as_column(index), 0, 3 * tile, pick_ref)
        picked = jnp.zeros((index.shape[1], c_own.shape[1]), jnp.float32)
        for t, c_ref in enumerate((c_before, c_own, c_after)):
            picked += jnp.dot(
                pick_ref[:, t * tile : (t + 1) * tile], c_ref[...], preferred_element_type=jnp.float32
            )
        orbitals = jnp.dot(
            b_ref[:npts, :], picked.astype(jnp.bfloat16), preferred_element_type=jnp.float32
        )
        rho = 2.0 * jnp.sum(orbitals * orbitals, axis=1, keepdims=True)
        rho = jnp.broadcast_to(rho, (npts, lanes)).T[0:1, :]
        out_ref[pl.ds(lax.rem(col + n_col - k, n_col), 1), :] = rho


def potential_kernel(n_col, n_row, npts, where_ref, *refs):
    b_own = refs[:n_col]
    b_prev, b_next, rho_own, rho_prev, rho_next, out_ref, x_ref, list_ref, pick_ref = refs[n_col:]
    nlist = b_prev.shape[2]
    tile = out_ref.shape[1]
    blocks = out_ref.shape[0] // tile
    chunk = min(256, tile)
    row, col = where_ref[0], where_ref[1]
    out_ref[...] = jnp.zeros_like(out_ref)
    for shift, batches, rho_ref in (
        (0, b_own, rho_own),
        (-1, [b_prev.at[k] for k in range(n_col)], rho_prev),
        (1, [b_next.at[k] for k in range(n_col)], rho_next),
    ):
        source = lax.rem(row + n_row + shift, n_row)
        for k, b_ref in enumerate(batches):
            rho = rho_ref[pl.ds(lax.rem(col + n_col - k, n_col), 1), :]
            pot = weight_of(b_ref, npts) * (-slater_coef * jnp.exp(jnp.log(rho + 1.0) * (1.0 / 3.0)))
            pot_col = as_column(pot)
            basis = b_ref[:npts, :]
            pot_full = jnp.concatenate([pot_col] * (nlist // lanes), axis=1)
            scaled = (basis.astype(jnp.float32) * pot_full).astype(jnp.bfloat16)
            vblock = lax.dot_general(
                basis, scaled, (((0,), (0,)), ((), ())), preferred_element_type=jnp.float32
            ).astype(jnp.bfloat16)
            index = list_of(b_ref, npts).astype(jnp.int32)
            list_ref[:, k * nlist : (k + 1) * nlist] = jnp.broadcast_to(index, (8, nlist))
            one_hot_columns(as_column(index), row * tile, tile, pick_ref)
            x_ref[k * nlist : (k + 1) * nlist, :] = jnp.dot(
                vblock, pick_ref[...], preferred_element_type=jnp.float32
            ).astype(jnp.bfloat16)
        for s in range(blocks):
            block = col * blocks + s
            inside = lax.rem(block - source + 1 + 2 * n_row, n_row) < 3

            @pl.when(inside)
            def _(block=block, s=s):
                def add(step, carry):
                    spot = lax.broadcasted_iota(jnp.int32, (chunk, list_ref.shape[1]), 0) + (
                        block * tile + step * chunk
                    )
                    place = jnp.where(list_ref[0:1, :] == spot, 1.0, 0.0).astype(jnp.bfloat16)
                    rows = pl.ds(pl.multiple_of(s * tile + step * chunk, chunk), chunk)
                    out_ref[rows, :] += jnp.dot(
                        place, x_ref[...], preferred_element_type=jnp.float32
                    )
                    return carry

                lax.fori_loop(0, tile // chunk, add, 0)


def density_kernel(n_col, where_ref, panel_ref, *refs):
    own_refs, out_ref = refs[:n_col], refs[n_col]
    col = where_ref[1]
    total = None
    for k, own_ref in enumerate(own_refs):
        group = latin(col, lax.rem(col + n_col - k, n_col), n_col)
        part = lax.dot_general(
            panel_ref[group], own_ref[...], (((1,), (1,)), ((), ())), preferred_element_type=jnp.float32
        )
        total = part if total is None else total + part
    out_ref[...] = (2.0 * total).astype(out_ref.dtype)


def on_device(coeffs, basis_values, point_weights, point_counts, func_lists):
    n_row, n_col = lax.axis_size("row"), lax.axis_size("col")
    tile, width = coeffs.shape
    blocks = n_row // n_col
    npts, nlist = basis_values.shape[1:]
    row, col = lax.axis_index("row"), lax.axis_index("col")
    where = jnp.stack([row, col]).astype(jnp.int32)

    def device(r, c):
        return r * n_col + c

    live = jnp.arange(npts, dtype=jnp.int32) < point_counts[0]
    weights = jnp.where(live, point_weights[0], 0.0)
    w1 = weights.astype(jnp.bfloat16)
    rest = weights - w1.astype(jnp.float32)
    w2 = rest.astype(jnp.bfloat16)
    w3 = (rest - w2.astype(jnp.float32)).astype(jnp.bfloat16)
    lists = func_lists[0]
    tail = jnp.stack([(lists // 128).astype(jnp.bfloat16), (lists % 128).astype(jnp.bfloat16), w1, w2, w3])
    tail = jnp.pad(tail, ((0, extra - tail.shape[0]), (0, 0)))
    batch = jnp.concatenate([basis_values[0], tail], axis=0)

    batches = [batch]
    for _ in range(1, n_col):
        batches.append(ring(batches[-1], n_col))
    before = row_shift(coeffs, n_row, 1)
    after = row_shift(coeffs, n_row, -1)

    spread = []
    for r in range(n_row):
        for c in range(n_col):
            spread.append((device(r, c), device(latin(r // blocks, c, n_col) * blocks + r % blocks, c)))
    piece = lax.ppermute(coeffs, both, spread)
    lift = []
    for r in range(n_row):
        for c in range(n_col):
            lift.append((device(r, c), device(r, latin(r // blocks, c, n_col))))
    piece = lax.ppermute(piece, both, lift)
    panel = lax.all_gather(piece, "row", axis=0, tiled=True)
    panel = panel.reshape(n_col, blocks * tile, width)

    def neighbours(x, by):
        pairs = []
        for r in range(n_row):
            for c in range(n_col):
                source = (r + by) % n_row
                if any((c * blocks + s - source + 1) % n_row < 3 for s in range(blocks)):
                    pairs.append((device(source, c), device(r, c)))
        return lax.ppermute(x, both, pairs)

    row_batches = jnp.stack(batches)
    prev_batches = neighbours(row_batches, -1)
    next_batches = neighbours(row_batches, 1)

    own = [coeffs]
    for _ in range(1, n_col):
        own.append(ring(own[-1], n_col))

    smem = pl.BlockSpec(memory_space=pltpu.SMEM)
    vmem = pl.BlockSpec(memory_space=pltpu.VMEM)
    partial = pl.pallas_call(
        functools.partial(rho_kernel, n_col, n_row, npts),
        out_shape=jax.ShapeDtypeStruct((n_col, npts), jnp.float32),
        in_specs=[smem] + [vmem] * (n_col + 3),
        out_specs=vmem,
        scratch_shapes=[pltpu.VMEM((nlist, 3 * tile), jnp.bfloat16)],
        compiler_params=pltpu.CompilerParams(vmem_limit_bytes=vmem_bytes),
        cost_estimate=pl.CostEstimate(
            flops=2 * n_col * nlist * width * (3 * tile + npts), bytes_accessed=6 << 20, transcendentals=0
        ),
        name="rho_partial",
    )(where, *batches, before, coeffs, after)
    rho = lax.psum(partial, "col")
    rho_prev = row_shift(rho, n_row, 1)
    rho_next = row_shift(rho, n_row, -1)

    potential = pl.pallas_call(
        functools.partial(potential_kernel, n_col, n_row, npts),
        out_shape=jax.ShapeDtypeStruct((blocks * tile, tile), jnp.float32),
        in_specs=[smem] + [vmem] * (n_col + 5),
        out_specs=vmem,
        scratch_shapes=[
            pltpu.VMEM((n_col * nlist, tile), jnp.bfloat16),
            pltpu.VMEM((8, n_col * nlist), jnp.int32),
            pltpu.VMEM((nlist, tile), jnp.bfloat16),
        ],
        compiler_params=pltpu.CompilerParams(vmem_limit_bytes=vmem_bytes),
        cost_estimate=pl.CostEstimate(
            flops=6 * n_col * nlist * (nlist * npts + nlist * tile + blocks * tile * tile),
            bytes_accessed=16 << 20,
            transcendentals=0,
        ),
        name="potential",
    )(where, *batches, prev_batches, next_batches, rho, rho_prev, rho_next)

    chunk = min(256, tile)
    density = pl.pallas_call(
        functools.partial(density_kernel, n_col),
        out_shape=jax.ShapeDtypeStruct((blocks * tile, tile), jnp.bfloat16),
        grid_spec=pltpu.PrefetchScalarGridSpec(
            num_scalar_prefetch=1,
            grid=(blocks * tile // chunk,),
            in_specs=[pl.BlockSpec((n_col, chunk, width), lambda i, where: (0, i, 0))]
            + [pl.BlockSpec((tile, width), lambda i, where: (0, 0))] * n_col,
            out_specs=pl.BlockSpec((chunk, tile), lambda i, where: (i, 0)),
        ),
        compiler_params=pltpu.CompilerParams(vmem_limit_bytes=vmem_bytes),
        cost_estimate=pl.CostEstimate(
            flops=2 * blocks * tile * tile * width * n_col, bytes_accessed=16 << 20, transcendentals=0
        ),
        name="density",
    )(where, panel, *own)
    return density, potential


def solution(mesh):
    in_specs = (
        P("row", "col"),
        P(("row", "col"), None, None),
        P(("row", "col"), None),
        P(("row", "col")),
        P(("row", "col"), None),
    )
    out_specs = (P("col", "row"), P("col", "row"))
    return jax.shard_map(
        on_device, mesh=mesh, in_specs=in_specs, out_specs=out_specs, check_vma=False
    )
```

time: 2190 us -> 311 us (0.14)
  waiting for transfers between devices: 1890 us -> 106 us
  local copies, waits for them, and re-layouts: 125 us -> 1.05 us
  starting transfers between devices: 4.78 us -> 91.3 us
  matrix products: 79.4 us -> 0 us
  Pallas kernels: 0 us -> 69.2 us
  other arithmetic: 67.4 us -> 5.57 us
  blocking collectives: 0 us -> 22.4 us
    all_gather x2 -> x1, waiting for transfers between devices: 919 us -> 0.01 us  [on_device(): panel = lax.all_gather(piece, 'row', axis=0, tiled=True)]
    psum x3 -> x0, waiting for transfers between devices: 792 us -> none  [the longest x1 628 us: on_device(): summed = lax.psum(placed.astype(jnp.bfloat16), 'col').astype(jnp.float32)]
    gather x2 -> x0, local copies, waits for them, and re-layouts: 119 us -> none  [the longest x1 85.3 us: on_device(): dens_window = jnp.take(full_rows, window_global, axis=0)]
    ppermute x4 -> x14, starting transfers between devices: 4.52 us -> 91.3 us  [the longest x2 54 us: neighbours(): return lax.ppermute(x, both, pairs)]
    dot_general x7 -> x0, matrix products: 79.4 us -> none  [the longest x1 33.2 us: on_device(): jnp.dot(select_full, spread_cols, precision=lax.Precision.HIGHEST, prefer...]
    ppermute x4 -> x14, waiting for transfers between devices: 182 us -> 106 us  [the longest x6 64 us: ring(): return lax.ppermute(x, 'col', [(i, (i + by) % n) for i in range(n)])]
    pallas_call x0 -> x3, Pallas kernels: none -> 69.2 us  [the longest x1 43.5 us: on_device(): pl.pallas_call(functools.partial(potential_kernel, n_col, n_row, npts), o...]
    psum x0 -> x1, blocking collectives: none -> 22.4 us  [on_device(): rho = lax.psum(partial, 'col')]
  transfers between devices with their start and end apart: 9 -> 15, of which waited for: 8 -> 8; matrix products, arithmetic and copies ran while one was open for 0% -> 2% of each run, Pallas kernels for 0% -> 18%
where the time goes in v1:
time: 311 us; the launch traced here: 310 us
  waiting for transfers between devices  106 us (34%)
  starting transfers between devices  91.3 us (29%)
  Pallas kernels  69.2 us (22%)
  blocking collectives  22.4 us (7%)
  between operations  14.8 us (5%)
  other arithmetic  5.57 us (2%)
    ppermute x6, waiting for transfers between devices, ring(): return lax.ppermute(x, 'col', [(i, (i + by) % n) for i in range(n)])  64 us
    ppermute x2, starting transfers between devices, neighbours(): return lax.ppermute(x, both, pairs)  54 us
    pallas_call x1, Pallas kernels, on_device(): pl.pallas_call(functools.partial(potential_kernel, n_col, n_row, npts), o...  43.5 us
    ppermute x4, waiting for transfers between devices, row_shift(): return lax.ppermute(x, 'row', [(i, (i + by) % n) for i in range(n)])  41.9 us
    ppermute x6, starting transfers between devices, ring(): return lax.ppermute(x, 'col', [(i, (i + by) % n) for i in range(n)])  28.3 us
    psum x1, blocking collectives, on_device(): rho = lax.psum(partial, 'col')  22.4 us
    pallas_call x1, Pallas kernels, on_device(): pl.pallas_call(functools.partial(density_kernel, n_col), out_shape=jax.Sh...  14.3 us
    pallas_call x1, Pallas kernels, on_device(): pl.pallas_call(functools.partial(rho_kernel, n_col, n_row, npts), out_sha...  11.4 us
  transfers between devices with their start and end apart: 15, of which 8 were waited for; matrix products, arithmetic and copies ran while one was open for 2% of the time, Pallas kernels for 18%

profile of v1, /device:TPU:0, one launch (start us, length us, event | category | flops | bytes accessed | tf_op | source)
XLA Modules:
  0.0 310.3 jit_solution(9729591987138333529)
XLA Ops:
  7.2 0.0 all-gather.2.cloned.1.call-start
  7.2 1.9 collective-permute-start
  9.1 0.0 collective-permute-done
  9.1 0.7 collective-permute-start.1
  9.8 0.0 collective-permute-done.1
  9.8 0.0 copy-start.2
  9.8 1.0 copy-done.2
  10.8 0.0 all-gather.2.cloned.1.call-update
  11.5 0.7 fusion.5
  12.2 0.7 subtract_convert_fusion
  12.9 0.7 fusion.2
  13.6 0.7 fusion.3
  14.3 1.1 fusion.6
  15.4 28.2 %collective-permute-start.5 = (bf16[528,512]{1,0:T(8,128)(2,1)S(1)}, bf16[528,512]{1,0:T(8,128)(2,1)S(1)}, u32[]{:S(2)}, u32[]{:S(2)}) collective-permute-start(bf16[528,512]{1,0:T(8,128)(2,1)S(1)} %get-tuple-element.5.refs_0_), channel_id=1, source_target_pairs={{0,1},{1,2},{2,3},{3,0},{4,5},{5,6},{6,7},{7,4},{8,9},{9,10},{10,1... | collective-permute-start | bytes 1622024 | tf_op jit(solution)/shard_map/ppermute | solution.py:24
  43.6 14.3 %collective-permute-done.5.refs_1_ = bf16[528,512]{1,0:T(8,128)(2,1)S(1)} collective-permute-done((bf16[528,512]{1,0:T(8,128)(2,1)S(1)}, bf16[528,512]{1,0:T(8,128)(2,1)S(1)}, u32[]{:S(2)}, u32[]{:S(2)}) %collective-permute-start.5) | collective-permute-done | bytes 540704 | tf_op jit(solution)/shard_map/ppermute | solution.py:24
  58.0 0.0 collective-permute-start.6
  58.0 14.3 %collective-permute-done.6.refs_2_ = bf16[528,512]{1,0:T(8,128)(2,1)S(1)} collective-permute-done((bf16[528,512]{1,0:T(8,128)(2,1)S(1)}, bf16[528,512]{1,0:T(8,128)(2,1)S(1)}, u32[]{:S(2)}, u32[]{:S(2)}) %collective-permute-start.6) | collective-permute-done | bytes 540704 | tf_op jit(solution)/shard_map/ppermute | solution.py:24
  72.3 0.0 collective-permute-start.7
  72.3 13.4 %collective-permute-done.7.refs_3_ = bf16[528,512]{1,0:T(8,128)(2,1)S(1)} collective-permute-done((bf16[528,512]{1,0:T(8,128)(2,1)S(1)}, bf16[528,512]{1,0:T(8,128)(2,1)S(1)}, u32[]{:S(2)}, u32[]{:S(2)}) %collective-permute-start.7) | collective-permute-done | bytes 540704 | tf_op jit(solution)/shard_map/ppermute | solution.py:24
  85.6 0.0 copy-start.3
  85.6 1.6 pad_maximum_fusion
  87.3 0.0 copy-done.3
  87.3 52.1 %collective-permute-start.9 = (bf16[4,528,512]{2,1,0:T(8,128)(2,1)}, bf16[4,528,512]{2,1,0:T(8,128)(2,1)}, u32[]{:S(2)}, u32[]{:S(2)}) collective-permute-start(bf16[4,528,512]{2,1,0:T(8,128)(2,1)} %pad_maximum_fusion), channel_id=1, source_target_pairs={{4,0},{5,1},{8,4},{9,5},{13,9},{14,10},{17,13},{18,14},{22,18},{23... | collective-permute-start | bytes 6488072 | tf_op jit(solution)/shard_map/ppermute | solution.py:189
  139.3 1.9 collective-permute-start.8
  141.3 0.0 copy-done
  141.3 0.1 collective-permute-start.2
  141.4 0.1 collective-permute-start.10
  141.4 5.8 %collective-permute-start.11 = (bf16[1024,512]{1,0:T(8,128)(2,1)S(1)}, bf16[1024,512]{1,0:T(8,128)(2,1)}, u32[]{:S(2)}, u32[]{:S(2)}) collective-permute-start(bf16[1024,512]{1,0:T(8,128)(2,1)S(1)} %copy-done), channel_id=1, source_target_pairs={{0,28},{4,0},{8,4},{12,8},{16,12},{20,16},{24,20},{28,24},{1,29},{... | collective-permute-start | bytes 3145736 | tf_op jit(solution)/shard_map/ppermute | solution.py:28
  147.2 22.0 %collective-permute-done.2.refs_1_ = bf16[1024,512]{1,0:T(8,128)(2,1)} collective-permute-done((bf16[1024,512]{1,0:T(8,128)(2,1)S(1)}, bf16[1024,512]{1,0:T(8,128)(2,1)}, u32[]{:S(2)}, u32[]{:S(2)}) %collective-permute-start.2) | collective-permute-done | bytes 1048608 | tf_op jit(solution)/shard_map/ppermute | solution.py:24
  169.2 0.0 collective-permute-start.3
  169.2 0.1 pad_add_fusion.where_ref
  169.3 25.8 %collective-permute-done.10.refs_4_ = bf16[1024,512]{1,0:T(8,128)(2,1)} collective-permute-done((bf16[1024,512]{1,0:T(8,128)(2,1)S(1)}, bf16[1024,512]{1,0:T(8,128)(2,1)}, u32[]{:S(2)}, u32[]{:S(2)}) %collective-permute-start.10) | collective-permute-done | bytes 1048608 | tf_op jit(solution)/shard_map/ppermute | solution.py:28
  195.1 12.6 %collective-permute-done.11.refs_6_ = bf16[1024,512]{1,0:T(8,128)(2,1)} collective-permute-done((bf16[1024,512]{1,0:T(8,128)(2,1)S(1)}, bf16[1024,512]{1,0:T(8,128)(2,1)}, u32[]{:S(2)}, u32[]{:S(2)}) %collective-permute-start.11) | collective-permute-done | bytes 1048608 | tf_op jit(solution)/shard_map/ppermute | solution.py:28
  207.7 11.4 %rho_partial.1 = f32[4,512]{1,0:T(4,128)S(1)} custom-call(s32[2]{0:T(128)S(1)} %pad_add_fusion.where_ref, bf16[528,512]{1,0:T(8,128)(2,1)S(1)} %get-tuple-element.5.refs_0_, bf16[528,512]{1,0:T(8,128)(2,1)S(1)} %collective-permute-done.5.refs_1_, bf16[528,512]{1,0:T(8,128)(2,1)S(1)} %collective-permute-done.6.refs_2_, bf16[528,512]{1,0:T(8,128)(2,1)} %copy-done.3, ...), custom_call_target="tpu_custom_call" | custom-call | flops 7516192768 | bytes 6291456 | tf_op jit(solution)/shard_map/rho_partial/pallas_call | solution.py:201
  219.1 22.4 %psum.7.refs_6_ = f32[4,512]{1,0:T(4,128)S(1)} all-reduce(f32[4,512]{1,0:T(4,128)S(1)} %rho_partial.1), channel_id=1, replica_groups=mesh['row'=8,'col'=4] {'col'}, use_global_device_ids=true, to_apply=%region_0.1 | all-reduce | flops 2048 | bytes 16384 | tf_op jit(solution)/shard_map/psum | solution.py:213
  241.5 0.0 copy-start.1
  241.5 0.1 collective-permute-start.13
  241.6 0.5 collective-permute-start.12
  242.1 0.0 collective-permute-done.3.refs_2_
  242.1 0.0 collective-permute-start.4
  242.1 0.9 collective-permute-done.13.refs_8_
  242.9 2.7 collective-permute-done.12.refs_7_
  245.6 0.0 collective-permute-done.9.refs_5_
  245.6 0.0 collective-permute-done.8.refs_4_
  245.6 43.5 %potential.1 = f32[2048,1024]{1,0:T(8,128)} custom-call(s32[2]{0:T(128)S(1)} %pad_add_fusion.where_ref, bf16[528,512]{1,0:T(8,128)(2,1)S(1)} %get-tuple-element.5.refs_0_, bf16[528,512]{1,0:T(8,128)(2,1)S(1)} %collective-permute-done.5.refs_1_, bf16[528,512]{1,0:T(8,128)(2,1)S(1)} %collective-permute-done.6.refs_2_, bf16[528,512]{1,0:T(8,128)(2,1)} %copy-done.3, ...), custom_call_target="tpu_custom_call" | custom-call | flops 35433480192 | bytes 16777216 | tf_op jit(solution)/shard_map/potential/pallas_call | solution.py:217
  289.1 0.0 collective-permute-done.4.refs_3_
  289.1 0.0 copy-done.1
  289.1 14.3 %density.1 = bf16[2048,1024]{1,0:T(8,128)(2,1)} custom-call(s32[2]{0:T(128)S(1)} %pad_add_fusion.where_ref, bf16[4,2048,512]{2,1,0:T(8,128)(2,1)} %bitcast.16, bf16[1024,512]{1,0:T(8,128)(2,1)S(1)} %copy-done.1, bf16[1024,512]{1,0:T(8,128)(2,1)} %collective-permute-done.2.refs_1_, bf16[1024,512]{1,0:T(8,128)(2,1)} %collective-permute-done.3.refs_2_, ...), custom_call_target="tpu_custom_call" | custom-call | flops 8589934592 | bytes 16777216 | tf_op jit(solution)/shard_map/density/pallas_call | solution.py:237
  (3 shorter events, 0.0 us)
Async XLA Ops:
  7.2 281.9 %all-gather.2.cloned.1.call-start = ((), (), s32[]{:S(2)}) async-start(), calls=%async_computation | async-start | bytes 9437184 | tf_op jit(solution)/shard_map/all_gather | solution.py:179
  7.2 1.9 collective-permute-start
  9.1 0.7 collective-permute-start.1
  9.8 1.0 copy-start.2
  15.4 42.5 %collective-permute-start.5 = (bf16[528,512]{1,0:T(8,128)(2,1)S(1)}, bf16[528,512]{1,0:T(8,128)(2,1)S(1)}, u32[]{:S(2)}, u32[]{:S(2)}) collective-permute-start(bf16[528,512]{1,0:T(8,128)(2,1)S(1)} %get-tuple-element.5.refs_0_), channel_id=1, source_target_pairs={{0,1},{1,2},{2,3},{3,0},{4,5},{5,6},{6,7},{7,4},{8,9},{9,10},{10,1... | collective-permute-start | bytes 1622024 | tf_op jit(solution)/shard_map/ppermute | solution.py:24
  58.0 14.3 %collective-permute-start.6 = (bf16[528,512]{1,0:T(8,128)(2,1)S(1)}, bf16[528,512]{1,0:T(8,128)(2,1)S(1)}, u32[]{:S(2)}, u32[]{:S(2)}) collective-permute-start(bf16[528,512]{1,0:T(8,128)(2,1)S(1)} %collective-permute-done.5.refs_1_), channel_id=1, source_target_pairs={{0,1},{1,2},{2,3},{3,0},{4,5},{5,6},{6,7},{7,4},{8,9},{9,10},{10,1... | collective-permute-start | bytes 1622024 | tf_op jit(solution)/shard_map/ppermute | solution.py:24
  72.3 13.4 %collective-permute-start.7 = (bf16[528,512]{1,0:T(8,128)(2,1)S(1)}, bf16[528,512]{1,0:T(8,128)(2,1)S(1)}, u32[]{:S(2)}, u32[]{:S(2)}) collective-permute-start(bf16[528,512]{1,0:T(8,128)(2,1)S(1)} %collective-permute-done.6.refs_2_), channel_id=1, source_target_pairs={{0,1},{1,2},{2,3},{3,0},{4,5},{5,6},{6,7},{7,4},{8,9},{9,10},{10,1... | collective-permute-start | bytes 1622024 | tf_op jit(solution)/shard_map/ppermute | solution.py:24
  85.6 1.6 copy-start.3
  85.6 55.6 %copy-start = (bf16[1024,512]{1,0:T(8,128)(2,1)S(1)}, bf16[1024,512]{1,0:T(8,128)(2,1)}, u32[]{:S(2)}) copy-start(bf16[1024,512]{1,0:T(8,128)(2,1)} %refs_5_.1) | copy-start | bytes 3145732
  87.3 158.4 %collective-permute-start.9 = (bf16[4,528,512]{2,1,0:T(8,128)(2,1)}, bf16[4,528,512]{2,1,0:T(8,128)(2,1)}, u32[]{:S(2)}, u32[]{:S(2)}) collective-permute-start(bf16[4,528,512]{2,1,0:T(8,128)(2,1)} %pad_maximum_fusion), channel_id=1, source_target_pairs={{4,0},{5,1},{8,4},{9,5},{13,9},{14,10},{17,13},{18,14},{22,18},{23... | collective-permute-start | bytes 6488072 | tf_op jit(solution)/shard_map/ppermute | solution.py:189
  139.3 106.3 %collective-permute-start.8 = (bf16[4,528,512]{2,1,0:T(8,128)(2,1)}, bf16[4,528,512]{2,1,0:T(8,128)(2,1)}, u32[]{:S(2)}, u32[]{:S(2)}) collective-permute-start(bf16[4,528,512]{2,1,0:T(8,128)(2,1)} %pad_maximum_fusion), channel_id=1, source_target_pairs={{28,0},{31,3},{0,4},{3,7},{4,8},{5,9},{8,12},{9,13},{13,17},{14,18... | collective-permute-start | bytes 6488072 | tf_op jit(solution)/shard_map/ppermute | solution.py:189
  141.3 27.9 %collective-permute-start.2 = (bf16[1024,512]{1,0:T(8,128)(2,1)S(1)}, bf16[1024,512]{1,0:T(8,128)(2,1)}, u32[]{:S(2)}, u32[]{:S(2)}) collective-permute-start(bf16[1024,512]{1,0:T(8,128)(2,1)S(1)} %copy-done), channel_id=1, source_target_pairs={{0,1},{1,2},{2,3},{3,0},{4,5},{5,6},{6,7},{7,4},{8,9},{9,10},{10,1... | collective-permute-start | bytes 3145736 | tf_op jit(solution)/shard_map/ppermute | solution.py:24
  141.4 53.7 %collective-permute-start.10 = (bf16[1024,512]{1,0:T(8,128)(2,1)S(1)}, bf16[1024,512]{1,0:T(8,128)(2,1)}, u32[]{:S(2)}, u32[]{:S(2)}) collective-permute-start(bf16[1024,512]{1,0:T(8,128)(2,1)S(1)} %copy-done), channel_id=1, source_target_pairs={{0,4},{4,8},{8,12},{12,16},{16,20},{20,24},{24,28},{28,0},{1,5},{5... | collective-permute-start | bytes 3145736 | tf_op jit(solution)/shard_map/ppermute | solution.py:28
  141.4 66.3 %collective-permute-start.11 = (bf16[1024,512]{1,0:T(8,128)(2,1)S(1)}, bf16[1024,512]{1,0:T(8,128)(2,1)}, u32[]{:S(2)}, u32[]{:S(2)}) collective-permute-start(bf16[1024,512]{1,0:T(8,128)(2,1)S(1)} %copy-done), channel_id=1, source_target_pairs={{0,28},{4,0},{8,4},{12,8},{16,12},{20,16},{24,20},{28,24},{1,29},{... | collective-permute-start | bytes 3145736 | tf_op jit(solution)/shard_map/ppermute | solution.py:28
  169.2 72.8 %collective-permute-start.3 = (bf16[1024,512]{1,0:T(8,128)(2,1)}, bf16[1024,512]{1,0:T(8,128)(2,1)}, u32[]{:S(2)}, u32[]{:S(2)}) collective-permute-start(bf16[1024,512]{1,0:T(8,128)(2,1)} %collective-permute-done.2.refs_1_), channel_id=1, source_target_pairs={{0,1},{1,2},{2,3},{3,0},{4,5},{5,6},{6,7},{7,4},{8,9},{9,10},{10,1... | collective-permute-start | bytes 3145736 | tf_op jit(solution)/shard_map/ppermute | solution.py:24
  241.5 47.6 %copy-start.1 = (bf16[1024,512]{1,0:T(8,128)(2,1)S(1)}, bf16[1024,512]{1,0:T(8,128)(2,1)}, u32[]{:S(2)}) copy-start(bf16[1024,512]{1,0:T(8,128)(2,1)} %refs_5_.1) | copy-start | bytes 3145732
  241.5 1.4 collective-permute-start.13
  241.6 4.0 %collective-permute-start.12 = (f32[4,512]{1,0:T(4,128)S(1)}, f32[4,512]{1,0:T(4,128)S(1)}, u32[]{:S(2)}, u32[]{:S(2)}) collective-permute-start(f32[4,512]{1,0:T(4,128)S(1)} %psum.7.refs_6_), channel_id=1, source_target_pairs={{0,4},{4,8},{8,12},{12,16},{16,20},{20,24},{24,28},{28,0},{1,5},{5... | collective-permute-start | bytes 24584 | tf_op jit(solution)/shard_map/ppermute | solution.py:28
  242.1 47.0 %collective-permute-start.4 = (bf16[1024,512]{1,0:T(8,128)(2,1)}, bf16[1024,512]{1,0:T(8,128)(2,1)}, u32[]{:S(2)}, u32[]{:S(2)}) collective-permute-start(bf16[1024,512]{1,0:T(8,128)(2,1)} %collective-permute-done.3.refs_2_), channel_id=1, source_target_pairs={{0,1},{1,2},{2,3},{3,0},{4,5},{5,6},{6,7},{7,4},{8,9},{9,10},{10,1... | collective-permute-start | bytes 3145736 | tf_op jit(solution)/shard_map/ppermute | solution.py:24
Sparse Core Ops, SparseCore 0:
  11.0 155.0 all-gather.1

commit v2 on v1

v2 whole, which is shorter than its diff:
```python
import functools

import jax
import jax.numpy as jnp
from jax import lax
from jax.experimental import pallas as pl
from jax.experimental.pallas import tpu as pltpu
from jax.sharding import PartitionSpec as P

slater_coef = 0.9847450218426965
both = ("row", "col")
extra = 16
lanes = 128
vmem_bytes = 52 * 1024 * 1024


def after(x, *done):
    return lax.optimization_barrier((x,) + done)[0]


def ring(x, n, by=1):
    return lax.ppermute(x, "col", [(i, (i + by) % n) for i in range(n)])


def row_shift(x, n, by):
    return lax.ppermute(x, "row", [(i, (i + by) % n) for i in range(n)])


def as_column(row_vec, width=lanes):
    return jnp.broadcast_to(row_vec, (width, row_vec.shape[1])).T


def list_of(b_ref, npts):
    hi = b_ref[npts : npts + 1, :].astype(jnp.float32)
    lo = b_ref[npts + 1 : npts + 2, :].astype(jnp.float32)
    return hi * 128.0 + lo


def weight_of(b_ref, npts):
    w1 = b_ref[npts + 2 : npts + 3, :].astype(jnp.float32)
    w2 = b_ref[npts + 3 : npts + 4, :].astype(jnp.float32)
    w3 = b_ref[npts + 4 : npts + 5, :].astype(jnp.float32)
    return (w1 + w2) + w3


def one_hot_columns(column, base, width, out_ref):
    for at in range(0, width, lanes):
        spot = lax.broadcasted_iota(jnp.int32, column.shape, 1) + (base + at)
        out_ref[:, at : at + lanes] = jnp.where(column == spot, 1.0, 0.0).astype(jnp.bfloat16)


def rho_kernel(n_col, n_row, npts, where_ref, *refs):
    b_refs, (c_before, c_own, c_after, out_ref, pick_ref) = refs[:n_col], refs[n_col:]
    tile = c_own.shape[0]
    total = tile * n_row
    row, col = where_ref[0], where_ref[1]
    start = lax.rem(row + n_row - 1, n_row) * tile
    for k, b_ref in enumerate(b_refs):
        index = list_of(b_ref, npts).astype(jnp.int32) - start
        index = jnp.where(index < 0, index + total, index)
        one_hot_columns(as_column(index), 0, 3 * tile, pick_ref)
        picked = jnp.zeros((index.shape[1], c_own.shape[1]), jnp.float32)
        for t, c_ref in enumerate((c_before, c_own, c_after)):
            picked += jnp.dot(
                pick_ref[:, t * tile : (t + 1) * tile], c_ref[...], preferred_element_type=jnp.float32
            )
        orbitals = jnp.dot(
            b_ref[:npts, :], picked.astype(jnp.bfloat16), preferred_element_type=jnp.float32
        )
        rho = 2.0 * jnp.sum(orbitals * orbitals, axis=1, keepdims=True)
        rho = jnp.broadcast_to(rho, (npts, lanes)).T[0:1, :]
        out_ref[pl.ds(lax.rem(col + n_col - k, n_col), 1), :] = rho


def touches(block, source, n_row):
    return lax.rem(block - source + 1 + 2 * n_row, n_row) < 3


def columns_kernel(n_col, n_row, npts, shift, where_ref, b_ref, rho_ref, x_ref, list_ref, pick_ref):
    nlist = b_ref.shape[2]
    tile = x_ref.shape[1]
    blocks = n_row // n_col
    row, col = where_ref[0], where_ref[1]
    source = lax.rem(row + n_row + shift, n_row)
    used = touches(col * blocks, source, n_row)
    for s in range(1, blocks):
        used = jnp.logical_or(used, touches(col * blocks + s, source, n_row))

    @pl.when(used)
    def _():
        for k in range(n_col):
            rho = rho_ref[pl.ds(lax.rem(col + n_col - k, n_col), 1), :]
            weight = weight_of(b_ref.at[k], npts)
            pot = weight * (-slater_coef * jnp.exp(jnp.log(rho + 1.0) * (1.0 / 3.0)))
            pot_full = jnp.concatenate([as_column(pot)] * (nlist // lanes), axis=1)
            basis = b_ref[k, :npts, :]
            scaled = (basis.astype(jnp.float32) * pot_full).astype(jnp.bfloat16)
            vblock = lax.dot_general(
                basis, scaled, (((0,), (0,)), ((), ())), preferred_element_type=jnp.float32
            ).astype(jnp.bfloat16)
            index = list_of(b_ref.at[k], npts).astype(jnp.int32)
            list_ref[:, k * nlist : (k + 1) * nlist] = jnp.broadcast_to(index, (8, nlist))
            one_hot_columns(as_column(index), row * tile, tile, pick_ref)
            x_ref[k * nlist : (k + 1) * nlist, :] = jnp.dot(
                vblock, pick_ref[...], preferred_element_type=jnp.float32
            ).astype(jnp.bfloat16)


def rows_kernel(n_col, n_row, tile, where_ref, *refs):
    x_refs, list_refs, out_ref = refs[:3], refs[3:6], refs[6]
    blocks = n_row // n_col
    chunk = out_ref.shape[0]
    row, col = where_ref[0], where_ref[1]
    base = col * blocks * tile + pl.program_id(0) * chunk
    block = lax.div(base, tile)
    out_ref[...] = jnp.zeros_like(out_ref)
    for shift, x_ref, list_ref in zip((0, -1, 1), x_refs, list_refs):
        source = lax.rem(row + n_row + shift, n_row)

        @pl.when(touches(block, source, n_row))
        def _(x_ref=x_ref, list_ref=list_ref):
            spot = lax.broadcasted_iota(jnp.int32, (chunk, list_ref.shape[1]), 0) + base
            place = jnp.where(list_ref[0:1, :] == spot, 1.0, 0.0).astype(jnp.bfloat16)
            out_ref[...] += jnp.dot(place, x_ref[...], preferred_element_type=jnp.float32)


def density_kernel(n_col, where_ref, first_ref, rest_ref, *refs):
    own_refs, out_ref = refs[:n_col], refs[n_col]
    parts, _, rows, _ = rest_ref.shape
    for p in range(parts):
        at = slice(p * rows, (p + 1) * rows)
        total = None
        for k, own_ref in enumerate(own_refs):
            panel = first_ref[at, :] if k == 0 else rest_ref[p, k - 1]
            part = lax.dot_general(
                panel, own_ref[...], (((1,), (1,)), ((), ())), preferred_element_type=jnp.float32
            )
            total = part if total is None else total + part
        out_ref[at, :] = (2.0 * total).astype(out_ref.dtype)


def on_device(coeffs, basis_values, point_weights, point_counts, func_lists):
    n_row, n_col = lax.axis_size("row"), lax.axis_size("col")
    tile, width = coeffs.shape
    blocks = n_row // n_col
    npts, nlist = basis_values.shape[1:]
    row, col = lax.axis_index("row"), lax.axis_index("col")
    where = jnp.stack([row, col]).astype(jnp.int32)

    def device(r, c):
        return r * n_col + c

    live = jnp.arange(npts, dtype=jnp.int32) < point_counts[0]
    weights = jnp.where(live, point_weights[0], 0.0)
    w1 = weights.astype(jnp.bfloat16)
    rest = weights - w1.astype(jnp.float32)
    w2 = rest.astype(jnp.bfloat16)
    w3 = (rest - w2.astype(jnp.float32)).astype(jnp.bfloat16)
    index = func_lists[0]
    tail = jnp.stack([(index // 128).astype(jnp.bfloat16), (index % 128).astype(jnp.bfloat16), w1, w2, w3])
    tail = jnp.pad(tail, ((0, extra - tail.shape[0]), (0, 0)))
    batch = jnp.concatenate([basis_values[0], tail], axis=0)

    slice_all = lax.all_gather(coeffs, "row", axis=0, tiled=True)

    batches = [batch]
    for _ in range(1, n_col):
        batches.append(ring(batches[-1], n_col))

    own = [coeffs, ring(after(coeffs, batches[-1]), n_col)]

    def neighbours(x, by):
        pairs = []
        for r in range(n_row):
            for c in range(n_col):
                source = (r + by) % n_row
                if any((c * blocks + s - source + 1) % n_row < 3 for s in range(blocks)):
                    pairs.append((device(source, c), device(r, c)))
        return lax.ppermute(x, both, pairs)

    row_batches = after(jnp.stack(batches), slice_all)
    prev_batches = neighbours(row_batches, -1)
    next_batches = neighbours(row_batches, 1)

    smem = pl.BlockSpec(memory_space=pltpu.SMEM)
    vmem = pl.BlockSpec(memory_space=pltpu.VMEM)
    def blocks_of(shift):
        return pl.BlockSpec((tile, width), lambda i, where: (lax.rem(where[0] + n_row + shift, n_row), 0))

    def whole(*shape):
        return pl.BlockSpec(shape, lambda i, where: (0,) * len(shape))

    partial = pl.pallas_call(
        functools.partial(rho_kernel, n_col, n_row, npts),
        out_shape=jax.ShapeDtypeStruct((n_col, npts), jnp.float32),
        grid_spec=pltpu.PrefetchScalarGridSpec(
            num_scalar_prefetch=1,
            grid=(1,),
            in_specs=[whole(npts + extra, nlist)] * n_col + [blocks_of(-1), blocks_of(0), blocks_of(1)],
            out_specs=whole(n_col, npts),
            scratch_shapes=[pltpu.VMEM((nlist, 3 * tile), jnp.bfloat16)],
        ),
        compiler_params=pltpu.CompilerParams(vmem_limit_bytes=vmem_bytes),
        cost_estimate=pl.CostEstimate(
            flops=2 * n_col * nlist * width * (3 * tile + npts), bytes_accessed=6 << 20, transcendentals=0
        ),
        name="rho_partial",
    )(where, *batches, slice_all, slice_all, slice_all)
    rho = lax.psum(partial, "col")
    part = blocks * tile // n_row
    parts = []
    slices = after(slice_all, rho, own[1])
    for k in range(1, n_col):
        start = lax.rem(col + k, n_col) * (blocks * tile) + row * part
        parts.append(ring(lax.dynamic_slice_in_dim(slices, start, part, 0), n_col, k))
    panel = lax.all_gather(after(jnp.stack(parts), prev_batches, next_batches), "row", axis=0)

    rho_prev = row_shift(rho, n_row, 1)
    rho_next = row_shift(rho, n_row, -1)

    placed, lists = [], []
    for shift, batches_of, rho_of in (
        (0, row_batches, rho),
        (-1, prev_batches, rho_prev),
        (1, next_batches, rho_next),
    ):
        x, index = pl.pallas_call(
            functools.partial(columns_kernel, n_col, n_row, npts, shift),
            out_shape=[
                jax.ShapeDtypeStruct((n_col * nlist, tile), jnp.bfloat16),
                jax.ShapeDtypeStruct((8, n_col * nlist), jnp.int32),
            ],
            in_specs=[smem, vmem, vmem],
            out_specs=[vmem, vmem],
            scratch_shapes=[pltpu.VMEM((nlist, tile), jnp.bfloat16)],
            compiler_params=pltpu.CompilerParams(vmem_limit_bytes=vmem_bytes),
            cost_estimate=pl.CostEstimate(
                flops=2 * n_col * nlist * nlist * (npts + tile), bytes_accessed=6 << 20, transcendentals=0
            ),
            name="columns",
        )(where, batches_of, rho_of)
        placed.append(x)
        lists.append(index)
        if shift == 0:
            own.append(ring(after(own[-1], rho), n_col))
    for _ in range(3, n_col):
        own.append(ring(after(own[-1], placed[0], rho_prev, rho_next), n_col))

    chunk = min(256, tile)
    potential = pl.pallas_call(
        functools.partial(rows_kernel, n_col, n_row, tile),
        out_shape=jax.ShapeDtypeStruct((blocks * tile, tile), jnp.float32),
        grid_spec=pltpu.PrefetchScalarGridSpec(
            num_scalar_prefetch=1,
            grid=(blocks * tile // chunk,),
            in_specs=[whole(n_col * nlist, tile)] * 3 + [whole(8, n_col * nlist)] * 3,
            out_specs=pl.BlockSpec((chunk, tile), lambda i, where: (i, 0)),
        ),
        compiler_params=pltpu.CompilerParams(vmem_limit_bytes=vmem_bytes),
        cost_estimate=pl.CostEstimate(
            flops=5 * n_col * nlist * blocks * tile * tile, bytes_accessed=20 << 20, transcendentals=0
        ),
        name="rows",
    )(where, *placed, *lists)

    step = max(chunk // part, 1)
    density = pl.pallas_call(
        functools.partial(density_kernel, n_col),
        out_shape=jax.ShapeDtypeStruct((blocks * tile, tile), jnp.bfloat16),
        grid_spec=pltpu.PrefetchScalarGridSpec(
            num_scalar_prefetch=1,
            grid=(n_row // step,),
            in_specs=[
                pl.BlockSpec((step * part, width), lambda i, where: (where[1] * (n_row // step) + i, 0)),
                pl.BlockSpec((step, n_col - 1, part, width), lambda i, where: (i, 0, 0, 0)),
            ]
            + [whole(tile, width)] * n_col,
            out_specs=pl.BlockSpec((step * part, tile), lambda i, where: (i, 0)),
        ),
        compiler_params=pltpu.CompilerParams(vmem_limit_bytes=vmem_bytes),
        cost_estimate=pl.CostEstimate(
            flops=2 * blocks * tile * tile * width * n_col, bytes_accessed=16 << 20, transcendentals=0
        ),
        name="density",
    )(where, slice_all, panel, *own)
    return density, potential


def solution(mesh):
    in_specs = (
        P("row", "col"),
        P(("row", "col"), None, None),
        P(("row", "col"), None),
        P(("row", "col")),
        P(("row", "col"), None),
    )
    out_specs = (P("col", "row"), P("col", "row"))
    return jax.shard_map(
        on_device, mesh=mesh, in_specs=in_specs, out_specs=out_specs, check_vma=False
    )
```

time: 311 us -> 224 us (0.72)
  starting transfers between devices: 91.3 us -> 19.3 us
  waiting for transfers between devices: 106 us -> 82.6 us
  Pallas kernels: 69.2 us -> 81.2 us
  blocking collectives: 22.4 us -> 17.6 us
    ppermute x2, starting transfers between devices: 54 us -> 7.76 us  [neighbours(): return lax.ppermute(x, both, pairs)]
    ppermute x4 -> x2, waiting for transfers between devices: 41.9 us -> 0.01 us  [row_shift(): return lax.ppermute(x, 'row', [(i, (i + by) % n) for i in range(n)])]
    ppermute x6 -> x9, starting transfers between devices: 28.3 us -> 8.86 us  [ring(): return lax.ppermute(x, 'col', [(i, (i + by) % n) for i in range(n)])]
    ppermute x6 -> x9, waiting for transfers between devices: 64 us -> 76 us  [ring(): return lax.ppermute(x, 'col', [(i, (i + by) % n) for i in range(n)])]
    pallas_call x1 -> x4, Pallas kernels: 43.5 us -> 55.2 us  [the longest x1 32.2 us: on_device(): pl.pallas_call(functools.partial(rows_kernel, n_col, n_row, tile), out_sh...]
    all_gather x1 -> x2, waiting for transfers between devices: 0.01 us -> 5.9 us  [the longest x1 5.9 us: on_device(): slice_all = lax.all_gather(coeffs, 'row', axis=0, tiled=True)]
    psum x1, blocking collectives: 22.4 us -> 17.6 us  [on_device(): rho = lax.psum(partial, 'col')]
    ppermute x4 -> x2, starting transfers between devices: 6.41 us -> 2.64 us  [row_shift(): return lax.ppermute(x, 'row', [(i, (i + by) % n) for i in range(n)])]
  transfers between devices with their start and end apart: 15 -> 15, of which waited for: 8 -> 7; matrix products, arithmetic and copies ran while one was open for 2% -> 3% of each run, Pallas kernels for 18% -> 30%
where the time goes in v2:
time: 224 us; the launch traced here: 223 us
  waiting for transfers between devices  82.6 us (37%)
  Pallas kernels  81.2 us (36%)
  starting transfers between devices  19.3 us (9%)
  blocking collectives  17.6 us (8%)
  between operations  14.8 us (7%)
  other arithmetic  6.56 us (3%)
    ppermute x9, waiting for transfers between devices, ring(): return lax.ppermute(x, 'col', [(i, (i + by) % n) for i in range(n)])  76 us
    pallas_call x1, Pallas kernels, on_device(): pl.pallas_call(functools.partial(rows_kernel, n_col, n_row, tile), out_sh...  32.2 us
    pallas_call x3, Pallas kernels, on_device(): pl.pallas_call(functools.partial(columns_kernel, n_col, n_row, npts, shif...  23.1 us
    psum x1, blocking collectives, on_device(): rho = lax.psum(partial, 'col')  17.6 us
    pallas_call x1, Pallas kernels, on_device(): pl.pallas_call(functools.partial(density_kernel, n_col), out_shape=jax.Sh...  14.3 us
    pallas_call x1, Pallas kernels, on_device(): pl.pallas_call(functools.partial(rho_kernel, n_col, n_row, npts), out_sha...  11.7 us
    ppermute x9, starting transfers between devices, ring(): return lax.ppermute(x, 'col', [(i, (i + by) % n) for i in range(n)])  8.86 us
    ppermute x2, starting transfers between devices, neighbours(): return lax.ppermute(x, both, pairs)  7.76 us
  transfers between devices with their start and end apart: 15, of which 7 were waited for; matrix products, arithmetic and copies ran while one was open for 3% of the time, Pallas kernels for 30%

profile of v2, /device:TPU:0, one launch (start us, length us, event | category | flops | bytes accessed | tf_op | source)
XLA Modules:
  0.0 223.3 jit_solution(8935854675083248406)
XLA Ops:
  7.2 0.0 all-gather.4.cloned.1.call-start
  7.2 0.7 all-gather.4.cloned.1.call-update
  7.9 0.0 all-gather.6.cloned.1.call-start
  8.6 0.7 fusion.5
  9.3 0.7 fusion.2
  10.0 0.7 fusion.3
  10.7 0.7 subtract_convert_fusion
  11.4 1.1 fusion.6
  12.5 3.1 %collective-permute-start = (bf16[528,512]{1,0:T(8,128)(2,1)S(1)}, bf16[528,512]{1,0:T(8,128)(2,1)S(1)}, u32[]{:S(2)}, u32[]{:S(2)}) collective-permute-start(bf16[528,512]{1,0:T(8,128)(2,1)S(1)} %get-tuple-element.32.refs_0_), channel_id=1, source_target_pairs={{0,1},{1,2},{2,3},{3,0},{4,5},{5,6},{6,7},{7,4},{8,9},{9,10},{10,1... | collective-permute-start | bytes 1622024 | tf_op jit(solution)/shard_map/ppermute | solution.py:22
  15.6 14.3 %collective-permute-done.refs_1_ = bf16[528,512]{1,0:T(8,128)(2,1)S(1)} collective-permute-done((bf16[528,512]{1,0:T(8,128)(2,1)S(1)}, bf16[528,512]{1,0:T(8,128)(2,1)S(1)}, u32[]{:S(2)}, u32[]{:S(2)}) %collective-permute-start) | collective-permute-done | bytes 540704 | tf_op jit(solution)/shard_map/ppermute | solution.py:22
  29.9 0.0 collective-permute-start.1
  29.9 15.3 %collective-permute-done.1.refs_2_ = bf16[528,512]{1,0:T(8,128)(2,1)S(1)} collective-permute-done((bf16[528,512]{1,0:T(8,128)(2,1)S(1)}, bf16[528,512]{1,0:T(8,128)(2,1)S(1)}, u32[]{:S(2)}, u32[]{:S(2)}) %collective-permute-start.1) | collective-permute-done | bytes 540704 | tf_op jit(solution)/shard_map/ppermute | solution.py:22
  45.2 0.0 collective-permute-start.2
  45.2 14.3 %collective-permute-done.2.refs_3_ = bf16[528,512]{1,0:T(8,128)(2,1)S(1)} collective-permute-done((bf16[528,512]{1,0:T(8,128)(2,1)S(1)}, bf16[528,512]{1,0:T(8,128)(2,1)S(1)}, u32[]{:S(2)}, u32[]{:S(2)}) %collective-permute-start.2) | collective-permute-done | bytes 540704 | tf_op jit(solution)/shard_map/ppermute | solution.py:22
  59.5 1.6 pad_maximum_fusion.b_ref
  61.1 5.9 %all-gather.4.cloned.1.call-done.refs_4_.refs_5_.refs_6_.first_ref = bf16[8192,512]{1,0:T(8,128)(2,1)} async-done(((bf16[1024,512]{1,0:T(8,128)(2,1)}), bf16[8192,512]{1,0:T(8,128)(2,1)}) %all-gather.4.cloned.1.call-update) | async-done | bytes 8388624 | tf_op jit(solution)/shard_map/all_gather | solution.py:164
  67.0 2.2 collective-permute-start.7
  69.2 5.6 %collective-permute-start.8 = (bf16[4,528,512]{2,1,0:T(8,128)(2,1)}, bf16[4,528,512]{2,1,0:T(8,128)(2,1)}, u32[]{:S(2)}, u32[]{:S(2)}) collective-permute-start(bf16[4,528,512]{2,1,0:T(8,128)(2,1)} %pad_maximum_fusion.b_ref), channel_id=1, source_target_pairs={{4,0},{5,1},{8,4},{9,5},{13,9},{14,10},{17,13},{18,14},{22,18},{23... | collective-permute-start | bytes 6488072 | tf_op jit(solution)/shard_map/ppermute | solution.py:179
  74.8 0.0 copy-done
  74.8 0.1 collective-permute-start.3
  74.9 0.1 pad_add_fusion.where_ref
  75.0 11.7 %rho_partial.1 = f32[4,512]{1,0:T(4,128)S(1)} custom-call(s32[2]{0:T(128)S(1)} %pad_add_fusion.where_ref, bf16[528,512]{1,0:T(8,128)(2,1)S(1)} %get-tuple-element.32.refs_0_, bf16[528,512]{1,0:T(8,128)(2,1)S(1)} %collective-permute-done.refs_1_, bf16[528,512]{1,0:T(8,128)(2,1)S(1)} %collective-permute-done.1.refs_2_, bf16[528,512]{1,0:T(8,128)(2,1)} %copy-done.1, ...), custom_call_target="tpu_custom_call" | custom-call | flops 7516192768 | bytes 6291456 | tf_op jit(solution)/shard_map/rho_partial/pallas_call | solution.py:193
  86.7 17.6 %psum.7.rho_ref = f32[4,512]{1,0:T(4,128)S(1)} all-reduce(f32[4,512]{1,0:T(4,128)S(1)} %rho_partial.1), channel_id=1, replica_groups=mesh['row'=8,'col'=4] {'col'}, use_global_device_ids=true, to_apply=%region_0.1 | all-reduce | flops 2048 | bytes 16384 | tf_op jit(solution)/shard_map/psum | solution.py:209
  104.3 0.0 collective-permute-done.3.refs_1_
  104.3 1.2 constant_dynamic-slice_fusion.2
  105.4 0.1 collective-permute-start.6
  105.5 0.6 collective-permute-start.5
  106.1 1.4 collective-permute-start.4
  107.5 6.7 %collective-permute-done.6 = bf16[256,512]{1,0:T(8,128)(2,1)S(1)} collective-permute-done((bf16[256,512]{1,0:T(8,128)(2,1)S(1)}, bf16[256,512]{1,0:T(8,128)(2,1)S(1)}, u32[]{:S(2)}, u32[]{:S(2)}) %collective-permute-start.6) | collective-permute-done | bytes 262176 | tf_op jit(solution)/shard_map/ppermute | solution.py:22
  114.2 12.9 %collective-permute-done.5 = bf16[256,512]{1,0:T(8,128)(2,1)S(1)} collective-permute-done((bf16[256,512]{1,0:T(8,128)(2,1)S(1)}, bf16[256,512]{1,0:T(8,128)(2,1)S(1)}, u32[]{:S(2)}, u32[]{:S(2)}) %collective-permute-start.5) | collective-permute-done | bytes 262176 | tf_op jit(solution)/shard_map/ppermute | solution.py:22
  127.1 0.0 collective-permute-done.4
  127.1 1.0 pad_maximum_fusion.1
  128.1 0.0 collective-permute-done.7.b_ref
  128.1 0.0 collective-permute-done.8.b_ref
  128.1 0.0 all-gather.6.cloned.1.call-update
  128.1 1.2 collective-permute-start.9
  129.3 0.0 collective-permute-start.10
  129.3 2.6 %collective-permute-start.11 = (f32[4,512]{1,0:T(4,128)S(1)}, f32[4,512]{1,0:T(4,128)S(1)}, u32[]{:S(2)}, u32[]{:S(2)}) collective-permute-start(f32[4,512]{1,0:T(4,128)S(1)} %psum.7.rho_ref), channel_id=1, source_target_pairs={{0,28},{4,0},{8,4},{12,8},{16,12},{20,16},{24,20},{28,24},{1,29},{... | collective-permute-start | bytes 24584 | tf_op jit(solution)/shard_map/ppermute | solution.py:26
  131.9 7.8 %columns.3 = (bf16[2048,1024]{1,0:T(8,128)(2,1)}, s32[8,2048]{1,0:T(8,128)S(1)}) custom-call(s32[2]{0:T(128)S(1)} %pad_add_fusion.where_ref, bf16[4,528,512]{2,1,0:T(8,128)(2,1)} %pad_maximum_fusion.b_ref, f32[4,512]{1,0:T(4,128)S(1)} %psum.7.rho_ref), custom_call_target="tpu_custom_call" | custom-call | flops 3221225472 | bytes 6291456 | tf_op jit(solution)/shard_map/columns/pallas_call | solution.py:227
  139.7 0.0 collective-permute-done.10.rho_ref
  139.7 0.0 collective-permute-done.11.rho_ref
  139.7 12.5 %collective-permute-done.9.refs_2_ = bf16[1024,512]{1,0:T(8,128)(2,1)S(1)} collective-permute-done((bf16[1024,512]{1,0:T(8,128)(2,1)}, bf16[1024,512]{1,0:T(8,128)(2,1)S(1)}, u32[]{:S(2)}, u32[]{:S(2)}) %collective-permute-start.9) | collective-permute-done | bytes 1048608 | tf_op jit(solution)/shard_map/ppermute | solution.py:22
  152.2 2.5 %collective-permute-start.12 = (bf16[1024,512]{1,0:T(8,128)(2,1)S(1)}, bf16[1024,512]{1,0:T(8,128)(2,1)}, u32[]{:S(2)}, u32[]{:S(2)}) collective-permute-start(bf16[1024,512]{1,0:T(8,128)(2,1)S(1)} %collective-permute-done.9.refs_2_), channel_id=1, source_target_pairs={{0,1},{1,2},{2,3},{3,0},{4,5},{5,6},{6,7},{7,4},{8,9},{9,10},{10,1... | collective-permute-start | bytes 3145736 | tf_op jit(solution)/shard_map/ppermute | solution.py:22
  154.7 7.5 %columns.4 = (bf16[2048,1024]{1,0:T(8,128)(2,1)}, s32[8,2048]{1,0:T(8,128)S(1)}) custom-call(s32[2]{0:T(128)S(1)} %pad_add_fusion.where_ref, bf16[4,528,512]{2,1,0:T(8,128)(2,1)} %collective-permute-done.7.b_ref, f32[4,512]{1,0:T(4,128)S(1)} %collective-permute-done.10.rho_ref), custom_call_target="tpu_custom_call" | custom-call | flops 3221225472 | bytes 6291456 | tf_op jit(solution)/shard_map/columns/pallas_call | solution.py:227
  162.2 7.8 %columns.5 = (bf16[2048,1024]{1,0:T(8,128)(2,1)}, s32[8,2048]{1,0:T(8,128)S(1)}) custom-call(s32[2]{0:T(128)S(1)} %pad_add_fusion.where_ref, bf16[4,528,512]{2,1,0:T(8,128)(2,1)} %collective-permute-done.8.b_ref, f32[4,512]{1,0:T(4,128)S(1)} %collective-permute-done.11.rho_ref), custom_call_target="tpu_custom_call" | custom-call | flops 3221225472 | bytes 6291456 | tf_op jit(solution)/shard_map/columns/pallas_call | solution.py:227
  170.0 32.2 %rows.1 = f32[2048,1024]{1,0:T(8,128)} custom-call(s32[2]{0:T(128)S(1)} %pad_add_fusion.where_ref, bf16[2048,1024]{1,0:T(8,128)(2,1)} %get-tuple-element.19.refs_0_, bf16[2048,1024]{1,0:T(8,128)(2,1)} %get-tuple-element.21.refs_1_, bf16[2048,1024]{1,0:T(8,128)(2,1)} %get-tuple-element.22.refs_2_, s32[8,2048]{1,0:T(8,128)S(1)} %get-tuple-element.23.refs_3_, ...), custom_call_target="tpu_custom_call" | custom-call | flops 21474836480 | bytes 20971520 | tf_op jit(solution)/shard_map/rows/pallas_call | solution.py:250
  202.2 0.0 collective-permute-done.12.refs_3_
  202.2 14.3 %density.1 = bf16[2048,1024]{1,0:T(8,128)(2,1)} custom-call(s32[2]{0:T(128)S(1)} %pad_add_fusion.where_ref, bf16[8192,512]{1,0:T(8,128)(2,1)} %all-gather.4.cloned.1.call-done.refs_4_.refs_5_.refs_6_.first_ref, bf16[8,3,256,512]{3,2,1,0:T(8,128)(2,1)} %bitcast.22, bf16[1024,512]{1,0:T(8,128)(2,1)S(1)} %copy-done, ...), custom_call_target="tpu_custom_call" | custom-call | flops 8589934592 | bytes 16777216 | tf_op jit(solution)/shard_map/density/pallas_call | solution.py:267
  (7 shorter events, 0.0 us)
Async XLA Ops:
  7.2 59.8 %all-gather.4.cloned.1.call-start = ((), (), s32[]{:S(2)}) async-start(), calls=%async_computation | async-start | bytes 9437184 | tf_op jit(solution)/shard_map/all_gather | solution.py:164
  7.9 194.3 %all-gather.6.cloned.1.call-start = ((), (), s32[]{:S(2)}) async-start(), calls=%async_computation.1 | async-start | bytes 7077888 | tf_op jit(solution)/shard_map/all_gather | solution.py:216
  12.5 17.4 %collective-permute-start = (bf16[528,512]{1,0:T(8,128)(2,1)S(1)}, bf16[528,512]{1,0:T(8,128)(2,1)S(1)}, u32[]{:S(2)}, u32[]{:S(2)}) collective-permute-start(bf16[528,512]{1,0:T(8,128)(2,1)S(1)} %get-tuple-element.32.refs_0_), channel_id=1, source_target_pairs={{0,1},{1,2},{2,3},{3,0},{4,5},{5,6},{6,7},{7,4},{8,9},{9,10},{10,1... | collective-permute-start | bytes 1622024 | tf_op jit(solution)/shard_map/ppermute | solution.py:22
  29.9 15.3 %collective-permute-start.1 = (bf16[528,512]{1,0:T(8,128)(2,1)S(1)}, bf16[528,512]{1,0:T(8,128)(2,1)S(1)}, u32[]{:S(2)}, u32[]{:S(2)}) collective-permute-start(bf16[528,512]{1,0:T(8,128)(2,1)S(1)} %collective-permute-done.refs_1_), channel_id=1, source_target_pairs={{0,1},{1,2},{2,3},{3,0},{4,5},{5,6},{6,7},{7,4},{8,9},{9,10},{10,1... | collective-permute-start | bytes 1622024 | tf_op jit(solution)/shard_map/ppermute | solution.py:22
  45.2 14.3 %collective-permute-start.2 = (bf16[528,512]{1,0:T(8,128)(2,1)S(1)}, bf16[528,512]{1,0:T(8,128)(2,1)S(1)}, u32[]{:S(2)}, u32[]{:S(2)}) collective-permute-start(bf16[528,512]{1,0:T(8,128)(2,1)S(1)} %collective-permute-done.1.refs_2_), channel_id=1, source_target_pairs={{0,1},{1,2},{2,3},{3,0},{4,5},{5,6},{6,7},{7,4},{8,9},{9,10},{10,1... | collective-permute-start | bytes 1622024 | tf_op jit(solution)/shard_map/ppermute | solution.py:22
  59.5 1.6 copy-start.1
  59.5 15.3 %copy-start = (bf16[1024,512]{1,0:T(8,128)(2,1)S(1)}, bf16[1024,512]{1,0:T(8,128)(2,1)}, u32[]{:S(2)}) copy-start(bf16[1024,512]{1,0:T(8,128)(2,1)} %refs_0_.1) | copy-start | bytes 3145732
  67.0 61.1 %collective-permute-start.7 = (bf16[4,528,512]{2,1,0:T(8,128)(2,1)}, bf16[4,528,512]{2,1,0:T(8,128)(2,1)}, u32[]{:S(2)}, u32[]{:S(2)}) collective-permute-start(bf16[4,528,512]{2,1,0:T(8,128)(2,1)} %pad_maximum_fusion.b_ref), channel_id=1, source_target_pairs={{28,0},{31,3},{0,4},{3,7},{4,8},{5,9},{8,12},{9,13},{13,17},{14,18... | collective-permute-start | bytes 6488072 | tf_op jit(solution)/shard_map/ppermute | solution.py:179
  69.2 58.9 %collective-permute-start.8 = (bf16[4,528,512]{2,1,0:T(8,128)(2,1)}, bf16[4,528,512]{2,1,0:T(8,128)(2,1)}, u32[]{:S(2)}, u32[]{:S(2)}) collective-permute-start(bf16[4,528,512]{2,1,0:T(8,128)(2,1)} %pad_maximum_fusion.b_ref), channel_id=1, source_target_pairs={{4,0},{5,1},{8,4},{9,5},{13,9},{14,10},{17,13},{18,14},{22,18},{23... | collective-permute-start | bytes 6488072 | tf_op jit(solution)/shard_map/ppermute | solution.py:179
  74.8 29.5 %collective-permute-start.3 = (bf16[1024,512]{1,0:T(8,128)(2,1)S(1)}, bf16[1024,512]{1,0:T(8,128)(2,1)}, u32[]{:S(2)}, u32[]{:S(2)}) collective-permute-start(bf16[1024,512]{1,0:T(8,128)(2,1)S(1)} %copy-done), channel_id=1, source_target_pairs={{0,1},{1,2},{2,3},{3,0},{4,5},{5,6},{6,7},{7,4},{8,9},{9,10},{10,1... | collective-permute-start | bytes 3145736 | tf_op jit(solution)/shard_map/ppermute | solution.py:22
  105.4 8.8 %collective-permute-start.6 = (bf16[256,512]{1,0:T(8,128)(2,1)S(1)}, bf16[256,512]{1,0:T(8,128)(2,1)S(1)}, u32[]{:S(2)}, u32[]{:S(2)}) collective-permute-start(bf16[256,512]{1,0:T(8,128)(2,1)S(1)} %get-tuple-element.29), channel_id=1, source_target_pairs={{0,3},{1,0},{2,1},{3,2},{4,7},{5,4},{6,5},{7,6},{8,11},{9,8},{10,9... | collective-permute-start | bytes 786440 | tf_op jit(solution)/shard_map/ppermute | solution.py:22
  105.5 21.6 %collective-permute-start.5 = (bf16[256,512]{1,0:T(8,128)(2,1)S(1)}, bf16[256,512]{1,0:T(8,128)(2,1)S(1)}, u32[]{:S(2)}, u32[]{:S(2)}) collective-permute-start(bf16[256,512]{1,0:T(8,128)(2,1)S(1)} %get-tuple-element.30), channel_id=1, source_target_pairs={{0,2},{1,3},{2,0},{3,1},{4,6},{5,7},{6,4},{7,5},{8,10},{9,11},{10,... | collective-permute-start | bytes 786440 | tf_op jit(solution)/shard_map/ppermute | solution.py:22
  106.1 21.0 %collective-permute-start.4 = (bf16[256,512]{1,0:T(8,128)(2,1)S(1)}, bf16[256,512]{1,0:T(8,128)(2,1)S(1)}, u32[]{:S(2)}, u32[]{:S(2)}) collective-permute-start(bf16[256,512]{1,0:T(8,128)(2,1)S(1)} %get-tuple-element.28), channel_id=1, source_target_pairs={{0,1},{1,2},{2,3},{3,0},{4,5},{5,6},{6,7},{7,4},{8,9},{9,10},{10,1... | collective-permute-start | bytes 786440 | tf_op jit(solution)/shard_map/ppermute | solution.py:22
  128.1 24.1 %collective-permute-start.9 = (bf16[1024,512]{1,0:T(8,128)(2,1)}, bf16[1024,512]{1,0:T(8,128)(2,1)S(1)}, u32[]{:S(2)}, u32[]{:S(2)}) collective-permute-start(bf16[1024,512]{1,0:T(8,128)(2,1)} %collective-permute-done.3.refs_1_), channel_id=1, source_target_pairs={{0,1},{1,2},{2,3},{3,0},{4,5},{5,6},{6,7},{7,4},{8,9},{9,10},{10,1... | collective-permute-start | bytes 3145736 | tf_op jit(solution)/shard_map/ppermute | solution.py:22
  129.3 10.4 %collective-permute-start.10 = (f32[4,512]{1,0:T(4,128)S(1)}, f32[4,512]{1,0:T(4,128)S(1)}, u32[]{:S(2)}, u32[]{:S(2)}) collective-permute-start(f32[4,512]{1,0:T(4,128)S(1)} %psum.7.rho_ref), channel_id=1, source_target_pairs={{0,4},{4,8},{8,12},{12,16},{16,20},{20,24},{24,28},{28,0},{1,5},{5... | collective-permute-start | bytes 24584 | tf_op jit(solution)/shard_map/ppermute | solution.py:26
  129.3 10.4 %collective-permute-start.11 = (f32[4,512]{1,0:T(4,128)S(1)}, f32[4,512]{1,0:T(4,128)S(1)}, u32[]{:S(2)}, u32[]{:S(2)}) collective-permute-start(f32[4,512]{1,0:T(4,128)S(1)} %psum.7.rho_ref), channel_id=1, source_target_pairs={{0,28},{4,0},{8,4},{12,8},{16,12},{20,16},{24,20},{28,24},{1,29},{... | collective-permute-start | bytes 24584 | tf_op jit(solution)/shard_map/ppermute | solution.py:26
  152.2 10.0 %copy-start.2 = (bf16[1024,512]{1,0:T(8,128)(2,1)}, bf16[1024,512]{1,0:T(8,128)(2,1)S(1)}, u32[]{:S(2)}) copy-start(bf16[1024,512]{1,0:T(8,128)(2,1)S(1)} %collective-permute-done.9.refs_2_) | copy-start | bytes 3145732
  152.2 49.9 %collective-permute-start.12 = (bf16[1024,512]{1,0:T(8,128)(2,1)S(1)}, bf16[1024,512]{1,0:T(8,128)(2,1)}, u32[]{:S(2)}, u32[]{:S(2)}) collective-permute-start(bf16[1024,512]{1,0:T(8,128)(2,1)S(1)} %collective-permute-done.9.refs_2_), channel_id=1, source_target_pairs={{0,1},{1,2},{2,3},{3,0},{4,5},{5,6},{6,7},{7,4},{8,9},{9,10},{10,1... | collective-permute-start | bytes 3145736 | tf_op jit(solution)/shard_map/ppermute | solution.py:22
Sparse Core Ops, SparseCore 0:
  9.9 57.0 all-gather.3
  128.3 45.1 all-gather.5
